TPU v7x, 512 devices: a whole 4x4x16 slice. The times are simulated.
512 devices in a mesh: dp: 8 (over z_lo), mp: 64 (over z_hi, y, x, core).
Axes of the slice: x: 4, y: 4, z: 16 (z_hi: 2, z_lo: 8; z = z_hi * 8 + z_lo), core: 2. Of those that a mesh axis runs over, the one named last changes fastest.
Arguments:
- narrow_input: bfloat16 [25088, 320], P(('dp', 'mp')), may hold values from 0 to 2
- narrow_output: bfloat16 [25088, 320], P(('dp', 'mp')), may hold values from 0 to 2
- narrow_mask: int32 [25088, 320], P(('dp', 'mp')), may hold values 0 or 1
- wide_cotangent: bfloat16 [32, 14, 14, 2560], P('dp', None, None, 'mp'), may hold values from -6 to 6
- wide_mask: int32 [32, 14, 14, 2560], P('dp', None, None, 'mp'), may hold values 0 or 1
- narrow_weight: bfloat16 [3, 3, 320, 320], replicated, may hold values from -0.109375 to 0.109375
- wide_weight: bfloat16 [3, 3, 1280, 2560], P(None, None, None, 'mp'), may hold values from -0.0546875 to 0.0546875
Outputs:
- narrow_gradient: bfloat16 [3, 3, 320, 320], replicated
- wide_gradient: bfloat16 [3, 3, 1280, 2560], P(None, None, 'dp', 'mp')
- input_gradient: bfloat16 [25088, 320], P(('dp', 'mp'))
All inputs are finite; a program needn't handle non-finite values. No bound on the sum of `narrow_mask` or of `wide_mask` on one device may be relied on, other than what follows from the above.
Results may differ from a plain program's by a relative error of at most 0.012.
Values may be sent and summed in bfloat16 or wider, within the bound.
A program may use at most 128 MiB of HBM per device.

v0:
```python
import jax
import jax.numpy as jnp
from jax import lax
from jax.sharding import PartitionSpec as P


def from_behind(x, axis, by):
    size = lax.axis_size(axis)
    return lax.ppermute(x, axis, [(i, (i + by) % size) for i in range(size)])


def from_partner(block, axis, stride):
    count = lax.axis_size(axis)
    route = []
    for low in range(count):
        high = low | 1 << stride
        if high != low and high < count:
            route += [(low, high), (high, low)]
    return lax.ppermute(block, axis, route)


def padded(block, sides, width):
    for axis, dim in sides:
        count = lax.axis_size(axis)
        forward = [(i, i + 1) for i in range(count - 1)]
        forward.append((count - 1, 0))
        backward = [(target, source) for source, target in forward]
        low = lax.ppermute(
            lax.slice_in_dim(block, block.shape[dim] - width, None, axis=dim), axis, forward
        )
        high = lax.ppermute(lax.slice_in_dim(block, 0, width, axis=dim), axis, backward)
        block = jnp.concatenate([low, block, high], axis=dim)
    return block


def to_coarse(images):
    count, rows, cols, chans = images.shape
    grid = images.reshape(count, rows // 2, 2, cols // 2, 2, chans)
    return grid.transpose(0, 1, 3, 2, 4, 5).reshape(count, rows // 2, cols // 2, 4 * chans)


def to_fine(coarse):
    count, rows, cols, chans = coarse.shape
    grid = coarse.reshape(count, rows, cols, 2, 2, chans // 4)
    return grid.transpose(0, 1, 3, 2, 4, 5).reshape(count, 2 * rows, 2 * cols, chans // 4)


def pad_grid(images):
    return jnp.pad(images, ((0, 0), (1, 1), (1, 1), (0, 0)))


def contract_rows(left, right):
    return lax.dot_general(
        left, right, (((0,), (0,)), ((), ())), preferred_element_type=jnp.float32
    )


def contract_cols(left, right):
    return lax.dot_general(
        left, right, (((1,), (1,)), ((), ())), preferred_element_type=jnp.float32
    )


def rotate_rows(array, amount):
    return jnp.concatenate([array[amount:], array[:amount]], 0)


def local(
    narrow_input, narrow_output, narrow_mask, wide_cotangent, wide_mask, narrow_weight, wide_weight
):
    groups = lax.axis_size("dp")
    members = lax.axis_size("mp")
    images = wide_cotangent.shape[0]
    coarse_side = wide_cotangent.shape[1]
    fine_side = 2 * coarse_side
    out_share = wide_cotangent.shape[3]
    channels = narrow_input.shape[1]
    wide_width = 4 * channels
    pixels = narrow_input.shape[0]
    total_images = images * groups
    offset_rows = fine_side * fine_side // 2
    block_rows = images * fine_side * fine_side
    wide_tangent = wide_cotangent * wide_mask.astype(jnp.bfloat16)
    gathered = lax.all_gather(narrow_output, "mp", axis=0, tiled=True)
    head = from_behind(gathered[block_rows - offset_rows :], "dp", 1)
    group_rows = jnp.concatenate([head, gathered[: block_rows - offset_rows]], 0)
    wide_in = to_coarse(group_rows.reshape(images, fine_side, fine_side, channels))
    padded_in = pad_grid(wide_in)
    padded_tan = pad_grid(wide_tangent)
    flat_tan = wide_tangent.reshape(-1, out_share)
    wide_terms = []
    back_terms = jnp.zeros((images * coarse_side * coarse_side, wide_width), jnp.float32)
    for tap_row in range(3):
        for tap_col in range(3):
            source = padded_in[
                :, tap_row : tap_row + coarse_side, tap_col : tap_col + coarse_side, :
            ].reshape(-1, wide_width)
            wide_terms.append(contract_rows(source, flat_tan))
            moved = padded_tan[
                :,
                2 - tap_row : 2 - tap_row + coarse_side,
                2 - tap_col : 2 - tap_col + coarse_side,
                :,
            ].reshape(-1, out_share)
            back_terms = back_terms + contract_cols(moved, wide_weight[tap_row, tap_col])
    wide_part = jnp.stack(wide_terms).reshape(3, 3, wide_width, out_share)
    wide_part = wide_part.astype(jnp.bfloat16).astype(jnp.float32)
    group_index = lax.axis_index("dp")
    levels = groups.bit_length() - 1
    kept = wide_part
    for level in range(levels):
        bit_pos = levels - 1 - level
        half = kept.shape[2] // 2
        lower = kept[:, :, :half]
        upper = kept[:, :, half:]
        upper_side = group_index >> bit_pos & 1 == 1
        keep_part = jnp.where(upper_side, upper, lower)
        send_part = jnp.where(upper_side, lower, upper)
        kept = keep_part + from_partner(send_part.astype(jnp.bfloat16), "dp", bit_pos).astype(
            send_part.dtype
        )
    wide_gradient = (kept / total_images).astype(jnp.bfloat16)
    back_grid = back_terms.reshape(images, coarse_side, coarse_side, wide_width)
    share = lax.psum_scatter(back_grid, "mp", scatter_dimension=3, tiled=True).astype(jnp.bfloat16)
    whole = lax.all_gather(share, "mp", axis=3, tiled=True)
    fine_whole = rotate_rows(to_fine(whole).reshape(-1, channels), offset_rows)
    own_back = lax.dynamic_slice_in_dim(fine_whole, lax.axis_index("mp") * pixels, pixels, 0)
    borrowed = from_behind(own_back, "dp", -1)
    from_next = lax.axis_index("mp") * pixels >= block_rows - offset_rows
    narrow_back = jnp.where(from_next, borrowed, own_back)
    narrow_tangent = narrow_back * narrow_mask.astype(jnp.bfloat16)
    stacked = jnp.stack([narrow_input, narrow_tangent])
    margin = fine_side + 1
    rimmed = padded(stacked, ((("dp", "mp"), 1),), fine_side + 1)
    first_pixel = (lax.axis_index("dp") * members + lax.axis_index("mp")) * pixels
    position = first_pixel + offset_rows + jnp.arange(pixels, dtype=jnp.int32)
    pixel_row = position % (fine_side * fine_side) // fine_side
    column = position % fine_side
    narrow_terms = []
    input_gradient = jnp.zeros((pixels, channels), jnp.float32)
    zero_value = jnp.zeros((), jnp.bfloat16)
    for tap_row in range(3):
        for tap_col in range(3):
            offset = (tap_row - 1) * fine_side + (tap_col - 1)
            ahead_row = pixel_row + tap_row - 1
            ahead_col = column + tap_col - 1
            inside = (
                (ahead_row >= 0)
                & (ahead_row < fine_side)
                & (ahead_col >= 0)
                & (ahead_col < fine_side)
            )
            source = rimmed[0, margin + offset : margin + offset + pixels]
            masked = jnp.where(inside[:, None], narrow_tangent, zero_value)
            narrow_terms.append(contract_rows(source, masked))
            behind_row = pixel_row - tap_row + 1
            behind_col = column - tap_col + 1
            inside_back = (
                (behind_row >= 0)
                & (behind_row < fine_side)
                & (behind_col >= 0)
                & (behind_col < fine_side)
            )
            incoming = jnp.where(
                inside_back[:, None],
                rimmed[1, margin - offset : margin - offset + pixels],
                zero_value,
            )
            input_gradient = input_gradient + contract_cols(
                incoming, narrow_weight[tap_row, tap_col]
            )
    narrow_part = jnp.stack(narrow_terms).reshape(3, 3, channels, channels)
    narrow_total = lax.psum(narrow_part, ("dp", "mp"))
    narrow_gradient = (narrow_total / total_images).astype(jnp.bfloat16)
    return (narrow_gradient, wide_gradient, input_gradient.astype(jnp.bfloat16))


def solution(mesh):
    placed = (
        P(("dp", "mp"), None),
        P(("dp", "mp"), None),
        P(("dp", "mp"), None),
        P("dp", None, None, "mp"),
        P("dp", None, None, "mp"),
        P(),
        P(None, None, None, "mp"),
    )
    return jax.shard_map(
        local,
        mesh=mesh,
        in_specs=placed,
        out_specs=(P(), P(None, None, "dp", "mp"), P(("dp", "mp"), None)),
        check_vma=False,
    )
```

profile of v0, /device:TPU:6, one launch (start us, length us, event | category | flops | bytes accessed | tf_op | source)
XLA Modules:
  0.0 1574.2 jit_solution(7350827255032885054)
XLA Ops:
  7.2 1.1 convert_multiply_fusion
  15.8 2.6 convolution_add_fusion
  18.4 5.0 reshape.271
  23.5 580.4 %all-reduce.7 = bf16[4,14,14,1280]{3,2,1,0:T(8,128)(2,1)S(1)} all-reduce(f32[4,14,14,1280]{3,2,1,0:T(8,128)} %reshape.271), channel_id=2, replica_groups=mesh['dp'=8,'mp'=64] {'mp'}, use_global_device_ids=true, to_apply=%region_0.1.clone | all-reduce | flops 1003520 | bytes 6021120
  603.9 1.3 dynamic-slice
  606.0 1.2 copy.99
  609.8 298.7 %all-gather.4.cloned.1.call-done = bf16[4,14,14,1280]{2,0,1,3:T(4,128)(2,1)} async-done(((bf16[4,14,14,20]{2,0,1,3:T(4,128)(2,1)}), bf16[4,14,14,1280]{2,0,1,3:T(4,128)(2,1)}) %all-gather.4.cloned.1.call-update) | async-done | bytes 2007056 | tf_op jit(solution)/shard_map/all_gather | solution.py:125
  908.5 32.2 %copy.124 = bf16[4,14,14,2,2,320]{5,4,2,3,1,0:T(2,128)(2,1)} copy(bf16[4,14,14,2,2,320]{2,0,1,5,4,3:T(4,128)(2,1)} %bitcast.284) | data formatting | bytes 4014080 | tf_op jit(solution)/shard_map/transpose | solution.py:45
  940.7 5.1 reshape_reshape.6
  946.2 1.9 collective-permute-start
  948.7 3.4 collective-permute-done
  952.8 1.9 collective-permute-start.2
  954.7 2.4 collective-permute-start.1
  957.2 68.1 %all-gather.6.cloned.1.call-done = bf16[64,49,320]{2,1,0:T(8,128)(2,1)} async-done(((bf16[1,49,320]{2,1,0:T(8,128)(2,1)}), bf16[64,49,320]{2,1,0:T(8,128)(2,1)}) %all-gather.6.cloned.1.call-update) | async-done | bytes 2007056 | tf_op jit(solution)/shard_map/all_gather | solution.py:84
  1025.2 1.7 slice-done
  1026.9 2.4 reshape.280
  1029.5 2.1 collective-permute-start.3
  1032.5 1.2 fusion.142
  1033.7 1.2 convolution_add_fusion.14
  1035.0 1.2 convolution_add_fusion.13
  1036.1 1.1 fusion.130
  1037.2 1.1 fusion.129
  1038.3 1.1 fusion.128
  1039.4 1.1 fusion.127
  1040.5 1.1 fusion.126
  1042.7 1.1 fusion.124
  1043.8 1.1 fusion.123
  1044.9 1.1 fusion.122
  1046.0 1.8 fusion.136
  1047.8 1.2 convolution_add_fusion.12
  1049.1 1.9 pad_maximum_fusion
  1050.9 2.5 reshape_reshape.7
  1053.4 3.3 copy.125
  1056.7 2.8 reshape.275
  1059.5 3.6 reshape.289
  1063.1 2.5 fusion.69
  1071.5 3.5 collective-permute-start.4
  1075.1 1.2 fusion.131
  1076.3 1.2 convolution_add_fusion.10
  1077.5 40.1 %collective-permute-done.4 = bf16[3,3,640,40]{2,3,1,0:T(8,128)(2,1)S(1)} collective-permute-done((bf16[3,3,640,40]{2,3,1,0:T(8,128)(2,1)S(1)}, bf16[3,3,640,40]{2,3,1,0:T(8,128)(2,1)S(1)}, u32[]{:S(2)}, u32[]{:S(2)}) %collective-permute-start.4) | collective-permute-done | bytes 460832 | tf_op jit(solution)/shard_map/ppermute | solution.py:19
  1117.9 1.9 collective-permute-start.5
  1119.8 1.2 convolution_add_fusion.9
  1121.0 13.9 collective-permute-done.5
  1135.3 1.9 collective-permute-start.6
  1137.2 1.8 fusion.132
  1139.0 5.0 collective-permute-done.6
  1144.9 418.8 %all-reduce.6.cloned.1.call-done = f32[3,3,320,320]{3,2,1,0:T(8,128)} async-done(((f32[3,3,320,320]{3,2,1,0:T(8,128)}), f32[3,3,320,320]{3,2,1,0:T(8,128)}) %all-reduce.6.cloned.1.call-update) | async-done | bytes 3686416 | tf_op jit(solution)/shard_map/psum | solution.py:173
  1563.7 4.0 multiply_convert_fusion
  (98 shorter events, 21.1 us)
Async XLA Ops:
  7.2 901.3 %all-gather.4.cloned.1.call-start = ((), (), s32[]{:S(2)}) async-start(), calls=%async_computation | async-start | bytes 18636800 | tf_op jit(solution)/shard_map/all_gather | solution.py:125
  9.3 1.2 copy-start.2
  607.2 418.1 %all-gather.6.cloned.1.call-start = ((), (), s32[]{:S(2)}) async-start(), calls=%async_computation.2 | async-start | bytes 2795520 | tf_op jit(solution)/shard_map/all_gather | solution.py:84
  607.9 955.7 %all-reduce.6.cloned.1.call-start = ((), (), s32[]{:S(2)}) async-start(), calls=%async_computation.1 | async-start | bytes 8847360 | tf_op jit(solution)/shard_map/psum | solution.py:173
  945.8 6.3 copy-start.5
  945.9 6.3 copy-start.3
  946.2 5.9 collective-permute-start
  952.8 78.8 %collective-permute-start.2 = (bf16[2,29,320]{2,1,0:T(8,128)(2,1)}, bf16[2,29,320]{2,1,0:T(8,128)(2,1)}, u32[]{:S(2)}, u32[]{:S(2)}) collective-permute-start(bf16[2,29,320]{2,1,0:T(8,128)(2,1)} %get-tuple-element.13), channel_id=1, source_target_pairs={{1,0},{2,1},{3,2},{4,3},{5,4},{6,5},{7,6},{8,7},{9,8},{10,9},{11,1... | collective-permute-start | bytes 111368 | tf_op jit(solution)/shard_map/ppermute | solution.py:31
  954.7 76.9 %collective-permute-start.1 = (bf16[2,29,320]{2,1,0:T(8,128)(2,1)}, bf16[2,29,320]{2,1,0:T(8,128)(2,1)}, u32[]{:S(2)}, u32[]{:S(2)}) collective-permute-start(bf16[2,29,320]{2,1,0:T(8,128)(2,1)} %get-tuple-element.14), channel_id=1, source_target_pairs={{0,1},{1,2},{2,3},{3,4},{4,5},{5,6},{6,7},{7,8},{8,9},{9,10},{10,1... | collective-permute-start | bytes 111368 | tf_op jit(solution)/shard_map/ppermute | solution.py:28
  1025.2 1.7 slice-start
  1026.9 2.4 slice-start.1
  1029.3 5.6 copy-start.11
  1029.3 7.9 copy-start.6
  1029.3 9.0 copy-start.8
  1029.3 10.1 copy-start.12
  1029.4 12.2 copy-start.10
  1029.5 19.5 %collective-permute-start.3 = (bf16[392,320]{1,0:T(8,128)(2,1)S(1)}, bf16[392,320]{1,0:T(8,128)(2,1)S(1)}, u32[]{:S(2)}, u32[]{:S(2)}) collective-permute-start(bf16[392,320]{1,0:T(8,128)(2,1)S(1)} %reshape.279), channel_id=1, source_target_pairs={{0,64},{64,128},{128,192},{192,256},{256,320},{320,384},{384,448},... | collective-permute-start | bytes 752648 | tf_op jit(solution)/shard_map/ppermute | solution.py:9
  1032.5 11.2 copy-start.14
  1034.9 10.0 copy-start.13
  1063.1 2.5 copy-start.1
  1066.2 1.6 copy-start
  1071.3 3.8 copy-start.4
  1071.3 5.0 copy-start.9
  1071.5 48.3 %copy-start.7 = (pred[49]{0:T(512)(128)(4,1)S(1)}, pred[49]{0:T(512)(128)(4,1)}, u32[]{:S(2)}) copy-start(pred[49]{0:T(512)(128)(4,1)} %get-tuple-element.22) | copy-start | bytes 151
  1071.5 46.0 %collective-permute-start.4 = (bf16[3,3,640,40]{2,3,1,0:T(8,128)(2,1)S(1)}, bf16[3,3,640,40]{2,3,1,0:T(8,128)(2,1)S(1)}, u32[]{:S(2)}, u32[]{:S(2)}) collective-permute-start(bf16[3,3,640,40]{2,3,1,0:T(8,128)(2,1)S(1)} %select_convert_fusion), channel_id=1, source_target_pairs={{0,256},{256,0},{64,320},{320,64},{128,384},{384,128},{192,448},{4... | collective-permute-start | bytes 1382408 | tf_op jit(solution)/shard_map/ppermute | solution.py:19
  1117.9 17.0 %collective-permute-start.5 = (bf16[3,3,320,40]{2,3,1,0:T(8,128)(2,1)S(1)}, bf16[3,3,320,40]{2,3,1,0:T(8,128)(2,1)S(1)}, u32[]{:S(2)}, u32[]{:S(2)}) collective-permute-start(bf16[3,3,320,40]{2,3,1,0:T(8,128)(2,1)S(1)} %select_convert_fusion.1), channel_id=1, source_target_pairs={{0,128},{128,0},{64,192},{192,64},{256,384},{384,256},{320,448},{4... | collective-permute-start | bytes 691208 | tf_op jit(solution)/shard_map/ppermute | solution.py:19
  1135.3 8.7 collective-permute-start.6
Sparse Core Ops, SparseCore 0:
  607.3 301.1 all-gather.3
  913.0 112.1 all-gather.5
  1048.0 515.6 all-reduce.5
where the time goes:
time: 1580 us; the launch traced here: 1570 us
  waiting for transfers between devices  849 us (54%)
  blocking collectives  580 us (37%)
  local copies, waits for them, and re-layouts  63.7 us (4%)
  matrix products  37.8 us (2%)
  starting transfers between devices  15.8 us (1%)
    unnamed x1, blocking collectives  580 us
    psum x1, waiting for transfers between devices, local(): narrow_total = lax.psum(narrow_part, ('dp', 'mp'))  419 us
    all_gather x1, waiting for transfers between devices, local(): whole = lax.all_gather(share, 'mp', axis=3, tiled=True)  299 us
    all_gather x1, waiting for transfers between devices, local(): gathered = lax.all_gather(narrow_output, 'mp', axis=0, tiled=True)  68.1 us
    ppermute x3, waiting for transfers between devices, from_partner(): return lax.ppermute(block, axis, route)  59 us
    transpose x1, local copies, waits for them, and re-layouts, to_fine(): grid.transpose(0, 1, 3, 2, 4, 5)  32.2 us
  transfers between devices with their start and end apart: 10, of which 7 were waited for; matrix products, arithmetic and copies ran while one was open for 6% of the time, Pallas kernels for 0%

commit v1 on v0

v1 whole, which is shorter than its diff:
```python
import functools

import jax
import jax.numpy as jnp
import numpy as np
from jax import lax
from jax.experimental import pallas as pl
from jax.experimental.pallas import tpu as pltpu
from jax.sharding import PartitionSpec as P

BF = jnp.bfloat16
F32 = jnp.float32
MESH = pl.DeviceIdType.MESH
PLANE = [(dy, dx) for dy in range(4) for dx in range(4) if (dy, dx) != (0, 0)]
VMEM_BYTES = 48 * 1024 * 1024


def place():
    g = lax.axis_index("dp")
    m = lax.axis_index("mp")
    return g, m // 32, (m // 8) % 4, (m // 2) % 4, m % 2


def device(g, zh, y, x, c):
    return (g, ((zh * 4 + y) * 4 + x) * 2 + c)


def remote(src, dst, send_sem, recv_sem, target):
    return pltpu.make_async_remote_copy(
        src_ref=src,
        dst_ref=dst,
        send_sem=send_sem,
        recv_sem=recv_sem,
        device_id=target,
        device_id_type=MESH,
    )


def greet(barrier, target):
    pl.semaphore_signal(barrier, inc=1, device_id=target, device_id_type=MESH)


def mm(left, right):
    return jnp.dot(left, right, preferred_element_type=F32)


def row_member(g, zh, y, x, c, d):
    other = (2 * x + c + d) % 8
    return device(g, zh, y, other // 2, other % 2)


def coarse_from_fine():
    out = np.zeros((4, 128, 512), np.float32)
    for i in range(2):
        for j in range(2):
            for p in range(7):
                for q in range(14):
                    fine = (2 * p + i) * 28 + 2 * q + j
                    out[2 * i + j, p * 14 + q, (fine // 49) * 64 + fine % 49] = 1
    return out


def fine_from_coarse():
    out = np.zeros((448, 512), np.float32)
    for i in range(2):
        for j in range(2):
            for p in range(7):
                for q in range(14):
                    fine = (2 * p + i) * 28 + 2 * q + j
                    out[28 + fine, (2 * i + j) * 128 + p * 14 + q] = 1
            for q in range(14):
                spot = (2 * i + j) * 128 + 98 + q
                out[(0 if i == 1 else 420) + 2 * q + j, spot] = 1
    return out


def spread():
    out = np.zeros((2, 320, 640), np.float32)
    for k in range(320):
        out[0, k, k] = 1
        out[1, k, 320 + k] = 1
    return out


def gather_kernel(
    blk, perm, put, gath, halo, xall, mine, pair, row_s, row_r, halo_s, halo_r, z_s, z_r, pl_s, pl_r, co_s, co_r
):
    g, zh, y, x, c = place()
    j = 2 * x + c
    row = (g * 8 + zh * 4 + y) % 64
    odd = y % 2
    is13 = (zh == 1) & (y == 3)
    is03 = (zh == 0) & (y == 3)
    barrier = pltpu.get_barrier_semaphore()

    gives = jnp.where(odd == 0, j == 0, j == 7)
    near = (row + jnp.where(odd == 0, 63, 1)) % 64
    near_g, near_zh, near_y = near // 8, (near // 4) % 2, near % 4
    near_j = jnp.where(odd == 0, 7, 0)
    halo_source = device(near_g, near_zh, near_y, near_j // 2, near_j % 2)

    for d in range(1, 8):
        greet(barrier, row_member(g, zh, y, x, c, d))
    greet(barrier, halo_source)
    for dy, dx in PLANE:
        if dy != 0:
            greet(barrier, device(g, zh, (y + dy) % 4, (x + dx) % 4, c))
    greet(barrier, device(jnp.where(is03, (g + 7) % 8, g), 1 - zh, y, x, c))

    @pl.when(is13)
    def _():
        greet(barrier, device((g + 7) % 8, 1, 3, x, c))

    total = 7 + 12 + 1 + jnp.where(gives, 8, 0) + jnp.where(is13, 1, 0)
    pl.semaphore_wait(barrier, total)

    gath[j] = blk[...]
    row_copies = []
    for d in range(1, 8):
        copy = remote(blk, gath.at[j], row_s.at[d - 1], row_r.at[d - 1], row_member(g, zh, y, x, c, d))
        copy.start()
        row_copies.append(copy)

    def halo_copy(d):
        return remote(blk.at[1], halo, halo_s.at[d], halo_r, device(near_g, near_zh, near_y, d // 2, d % 2))

    @pl.when(gives)
    def _():
        for d in range(8):
            halo_copy(d).start()

    for copy in row_copies:
        copy.wait()

    part = jnp.zeros((32, 640), F32)
    for jj in range(2):
        acc = jnp.zeros((32, 320), F32)
        for b in range(8):
            sel = perm[2 * c + jj, pl.ds(pl.multiple_of(32 * x, 32), 32), 64 * b : 64 * b + 64]
            acc = acc + mm(sel, gath[b, 0])
        part = part + mm(acc.astype(BF), put[jj])
    mine[...] = part.astype(BF)

    z_a = remote(
        mine, pair.at[zh], z_s.at[0], z_r.at[0], device(jnp.where(is13, (g + 1) % 8, g), 1 - zh, y, x, c)
    )
    z_b = remote(mine, pair.at[1], z_s.at[1], z_r.at[1], device((g + 1) % 8, 1, 3, x, c))
    z_a.start()

    @pl.when(is13)
    def _():
        z_b.start()

    @pl.when(jnp.logical_not(is13))
    def _():
        pair[zh] = mine[...]

    z_a.wait()

    @pl.when(is13)
    def _():
        z_b.wait()

    xall[c, y, x] = pair[...]
    plane_copies = []
    for k, (dy, dx) in enumerate(PLANE):
        copy = remote(
            pair, xall.at[c, y, x], pl_s.at[k], pl_r.at[k], device(g, zh, (y + dy) % 4, (x + dx) % 4, c)
        )
        copy.start()
        plane_copies.append(copy)
    peer = device(g, zh, y, x, 1 - c)
    core_copies = []
    for k, (dy, dx) in enumerate([(0, 0)] + PLANE):
        if k > 0:
            plane_copies[k - 1].wait_recv()
        spot = xall.at[c, (y + 4 - dy) % 4, (x + 4 - dx) % 4]
        copy = remote(spot, spot, co_s.at[k], co_r.at[k], peer)
        copy.start()
        core_copies.append(copy)
    for copy in plane_copies:
        copy.wait_send()
    for copy in core_copies:
        copy.wait()
    halo_copy(0).wait_recv()

    @pl.when(gives)
    def _():
        for d in range(8):
            halo_copy(d).wait_send()


def gather_call(blk):
    vm = pl.BlockSpec(memory_space=pltpu.VMEM)
    return pl.pallas_call(
        gather_kernel,
        out_shape=(
            jax.ShapeDtypeStruct((8, 3, 64, 320), BF),
            jax.ShapeDtypeStruct((64, 320), BF),
            jax.ShapeDtypeStruct((2, 4, 4, 2, 32, 640), BF),
        ),
        in_specs=[vm] * 3,
        out_specs=(vm, vm, vm),
        scratch_shapes=[
            pltpu.VMEM((32, 640), BF),
            pltpu.VMEM((2, 32, 640), BF),
            pltpu.SemaphoreType.DMA((7,)),
            pltpu.SemaphoreType.DMA((7,)),
            pltpu.SemaphoreType.DMA((8,)),
            pltpu.SemaphoreType.DMA,
            pltpu.SemaphoreType.DMA((2,)),
            pltpu.SemaphoreType.DMA((2,)),
            pltpu.SemaphoreType.DMA((15,)),
            pltpu.SemaphoreType.DMA((15,)),
            pltpu.SemaphoreType.DMA((16,)),
            pltpu.SemaphoreType.DMA((16,)),
        ],
        compiler_params=pltpu.CompilerParams(
            collective_id=0, has_side_effects=True, vmem_limit_bytes=VMEM_BYTES
        ),
        name="gather_rows",
    )(blk, jnp.asarray(coarse_from_fine(), BF), jnp.asarray(spread(), BF))


def reduce_kernel(
    tcol, w, nb, psend, precv, part, rbuf, acc, zsend, zrecv, co_s, co_r, pl_s, pl_r, z_s, z_r, row_s, row_r
):
    g, zh, y, x, c = place()
    is13 = (zh == 1) & (y == 3)
    is03 = (zh == 0) & (y == 3)
    peer = device(g, zh, y, x, 1 - c)
    barrier = pltpu.get_barrier_semaphore()
    for d in range(1, 8):
        greet(barrier, row_member(g, zh, y, x, c, d))
    for dy, dx in PLANE:
        if dy != 0:
            greet(barrier, device(g, zh, (y + dy) % 4, (x + dx) % 4, c))
    greet(barrier, device(jnp.where(is13, (g + 1) % 8, g), 1 - zh, y, x, c))

    @pl.when(is13)
    def _():
        greet(barrier, device((g + 1) % 8, 1, 3, x, c))

    pl.semaphore_wait(barrier, 7 + 12 + 1 + jnp.where(is13, 1, 0))

    theirs = pl.ds(pl.multiple_of((1 - c) * 640, 128), 640)
    ours = pl.ds(pl.multiple_of(c * 640, 128), 640)
    core_copies = []
    for dy in (1, 2, 3, 0):
        yy = (y + dy) % 4
        psend[yy] = mm(tcol[yy], w[:, theirs]).astype(BF)
        copy = remote(psend.at[yy], precv.at[yy], co_s.at[dy], co_r.at[dy], peer)
        copy.start()
        core_copies.append(copy)
    plane_copies = []
    for n, dy in enumerate((1, 2, 3, 0)):
        yy = (y + dy) % 4
        own = mm(tcol[yy], w[:, ours])
        core_copies[n].wait_recv()
        part[yy] = (own + precv[yy].astype(F32)).astype(BF).reshape(4, 2, 32, 640)
        for dx in range(4):
            if (dy, dx) == (0, 0):
                continue
            k = PLANE.index((dy, dx))
            xx = (x + dx) % 4
            copy = remote(part.at[yy, xx], rbuf.at[k], pl_s.at[k], pl_r.at[k], device(g, zh, yy, xx, c))
            copy.start()
            plane_copies.append((k, copy))
    acc[...] = part[y, x].astype(F32)
    for k, copy in plane_copies:
        copy.wait_recv()
        acc[...] += rbuf[k].astype(F32)
    zsend[...] = acc[...].astype(BF)
    z_a = remote(
        zsend.at[1 - zh],
        zrecv.at[zh],
        z_s.at[0],
        z_r.at[0],
        device(jnp.where(is03, (g + 7) % 8, g), 1 - zh, y, x, c),
    )
    z_b = remote(zsend.at[1], zrecv.at[1], z_s.at[1], z_r.at[1], device((g + 7) % 8, 1, 3, x, c))
    z_a.start()

    @pl.when(is13)
    def _():
        z_b.start()

    for copy in core_copies:
        copy.wait_send()
    for k, copy in plane_copies:
        copy.wait_send()
    z_a.wait()

    @pl.when(is13)
    def _():
        z_b.wait()
        nb[c, x] = (zrecv[0].astype(F32) + zrecv[1].astype(F32)).astype(BF)

    @pl.when(jnp.logical_not(is13))
    def _():
        nb[c, x] = (acc[zh] + zrecv[1 - zh].astype(F32)).astype(BF)

    row_copies = []
    for d in range(1, 8):
        copy = remote(
            nb.at[c, x], nb.at[c, x], row_s.at[d - 1], row_r.at[d - 1], row_member(g, zh, y, x, c, d)
        )
        copy.start()
        row_copies.append(copy)
    for copy in row_copies:
        copy.wait()


def reduce_call(tcol, w):
    vm = pl.BlockSpec(memory_space=pltpu.VMEM)
    return pl.pallas_call(
        reduce_kernel,
        out_shape=jax.ShapeDtypeStruct((2, 4, 32, 640), BF),
        in_specs=[vm] * 2,
        out_specs=vm,
        scratch_shapes=[
            pltpu.VMEM((4, 256, 640), BF),
            pltpu.VMEM((4, 256, 640), BF),
            pltpu.VMEM((4, 4, 2, 32, 640), BF),
            pltpu.VMEM((15, 2, 32, 640), BF),
            pltpu.VMEM((2, 32, 640), F32),
            pltpu.VMEM((2, 32, 640), BF),
            pltpu.VMEM((2, 32, 640), BF),
            pltpu.SemaphoreType.DMA((4,)),
            pltpu.SemaphoreType.DMA((4,)),
            pltpu.SemaphoreType.DMA((15,)),
            pltpu.SemaphoreType.DMA((15,)),
            pltpu.SemaphoreType.DMA((2,)),
            pltpu.SemaphoreType.DMA((2,)),
            pltpu.SemaphoreType.DMA((7,)),
            pltpu.SemaphoreType.DMA((7,)),
        ],
        compiler_params=pltpu.CompilerParams(
            collective_id=1, has_side_effects=True, vmem_limit_bytes=VMEM_BYTES
        ),
        name="reduce_back",
    )(tcol, w)


def narrow_kernel(nb, mask, inj, wn, perm, pull, s_out, ig_out, nt, s_acc):
    j = lax.axis_index("mp") % 8
    fine = jnp.zeros((448, 320), F32)
    for i in range(2):
        for jj in range(2):
            spot = (2 * i + jj) * 128
            block = mm(nb[i], pull[jj]).astype(BF)
            fine = fine + mm(perm[:, spot : spot + 128], block)
    nt[...] = jnp.zeros_like(nt)
    nt[8:456, :] = fine * mask[...].astype(F32)
    pixel = lax.broadcasted_iota(jnp.int32, (392, 320), 0)
    column = pixel % 28
    rows = lax.broadcasted_iota(jnp.int32, (64, 392), 0)
    cols = lax.broadcasted_iota(jnp.int32, (64, 392), 1)
    mine = jnp.where((cols == rows + 49 * j) & (rows < 49), 1.0, 0.0).astype(BF)
    ig = jnp.zeros((64, 320), F32)
    s_acc[...] = jnp.zeros_like(s_acc)
    for t in range(9):
        dr, dc = 1 - t // 3, 1 - t % 3
        start = 8 + 28 + 28 * dr + dc
        moved = nt[start : start + 392, :]
        if dc == -1:
            moved = jnp.where(column >= 1, moved, 0.0)
        if dc == 1:
            moved = jnp.where(column <= 26, moved, 0.0)
        moved = moved.astype(BF)
        s_acc[40 * t : 40 * t + 40, :] = lax.dot_general(
            inj[...], moved, (((0,), (0,)), ((), ())), preferred_element_type=F32
        )
        own = mm(mine, moved).astype(BF)
        ig = ig + lax.dot_general(own, wn[t], (((1,), (1,)), ((), ())), preferred_element_type=F32)
    s_out[...] = s_acc[...].astype(BF)
    ig_out[...] = ig.astype(BF)


def pull():
    return spread().transpose(0, 2, 1)


def narrow_call(nb, mask, inj, wn):
    vm = pl.BlockSpec(memory_space=pltpu.VMEM)
    return pl.pallas_call(
        narrow_kernel,
        out_shape=(jax.ShapeDtypeStruct((384, 320), BF), jax.ShapeDtypeStruct((64, 320), BF)),
        in_specs=[vm] * 6,
        out_specs=(vm, vm),
        scratch_shapes=[pltpu.VMEM((464, 320), F32), pltpu.VMEM((384, 320), F32)],
        compiler_params=pltpu.CompilerParams(vmem_limit_bytes=VMEM_BYTES),
        name="narrow_local",
    )(nb, mask, inj, wn, jnp.asarray(fine_from_coarse(), BF), jnp.asarray(pull(), BF))


def holder(k):
    return (8 * k) // 3


def finish_kernel(
    s_in,
    wide,
    ng,
    wg,
    ybuf,
    zpart,
    zbuf,
    zfin,
    wbuf,
    w_s,
    w_r,
    y_s,
    y_r,
    z_s,
    z_r,
    b_s,
    b_r,
    pl_s,
    pl_r,
    co_s,
    co_r,
):
    g, zh, y, x, c = place()
    zz = zh * 8 + g
    j = 2 * x + c
    peer = device(g, zh, y, x, 1 - c)

    def along(d):
        other = (zz + d) % 16
        return device(other % 8, other // 8, y, x, c)

    barrier = pltpu.get_barrier_semaphore()
    for dy, dx in PLANE:
        greet(barrier, device(g, zh, (y + dy) % 4, (x + dx) % 4, c))
    for d in range(1, 16):
        greet(barrier, along(d))
    greet(barrier, peer)
    pl.semaphore_wait(barrier, 31)

    wide_copies = []
    for d in range(1, 8):
        gg = (g + d) % 8
        copy = remote(wide.at[gg], wbuf.at[d - 1], w_s.at[d - 1], w_r.at[d - 1], device(gg, zh, y, x, c))
        wide_copies.append(copy)

    y_copies = []
    for d in range(1, 4):
        yy = (y + d) % 4
        copy = remote(s_in.at[yy], ybuf.at[d - 1], y_s.at[d - 1], y_r.at[d - 1], device(g, zh, yy, x, c))
        copy.start()
        y_copies.append(copy)
    total = s_in[y].astype(F32)
    for copy, d in zip(y_copies, range(3)):
        copy.wait_recv()
        total = total + ybuf[d].astype(F32)
    zpart[...] = total.astype(BF)

    def z_copy(k, d):
        return remote(
            zpart.at[pl.ds(16 * k, 16)],
            zbuf.at[d - 1],
            z_s.at[k],
            z_r.at[d - 1],
            along(d),
        )

    for k in range(6):
        d = (holder(k) - zz + 16) % 16

        @pl.when(d != 0)
        def _():
            z_copy_to(zpart, zbuf, z_s, z_r, k, d, along).start()

    def back_copy(k, d):
        return remote(
            zfin.at[pl.ds(16 * k, 16)],
            zfin.at[pl.ds(16 * k, 16)],
            b_s.at[d - 1],
            b_r.at[k],
            along(d),
        )

    for k in range(6):

        @pl.when(zz == holder(k))
        def _():
            value = zpart[16 * k : 16 * k + 16, :].astype(F32)
            for d in range(1, 16):
                z_copy(k, d).wait_recv()
                value = value + zbuf[d - 1].astype(F32)
            zfin[16 * k : 16 * k + 16, :] = (value * (1.0 / 32.0)).astype(BF)
            for d in range(1, 16):
                back_copy(k, d).start()

    for copy in wide_copies:
        copy.start()

    for k in range(6):

        @pl.when(zz != holder(k))
        def _():
            back_copy(k, 1).wait_recv()

    plane_copies = []
    for k, (dy, dx) in enumerate(PLANE):
        copy = remote(
            zfin, ng.at[j, y], pl_s.at[k], pl_r.at[k], device(g, zh, (y + dy) % 4, (x + dx) % 4, c)
        )
        copy.start()
        plane_copies.append(copy)
    ng[j, y] = zfin[...]
    core_copies = []
    for k, (dy, dx) in enumerate([(0, 0)] + PLANE):
        if k > 0:
            plane_copies[k - 1].wait_recv()
        spot = ng.at[2 * ((x + 4 - dx) % 4) + c, (y + 4 - dy) % 4]
        copy = remote(spot, spot, co_s.at[k], co_r.at[k], peer)
        copy.start()
        core_copies.append(copy)

    terms = wide[g].astype(F32)
    for d in range(7):
        wide_copies[d].wait_recv()
        terms = terms + wbuf[d].astype(F32)
    wg[...] = (terms * (1.0 / 32.0)).astype(BF)

    for copy in y_copies + wide_copies + plane_copies:
        copy.wait_send()
    for k in range(6):

        @pl.when(zz != holder(k))
        def _():
            z_copy(k, 1).wait_send()

        @pl.when(zz == holder(k))
        def _():
            for d in range(1, 16):
                back_copy(k, d).wait_send()

    for copy in core_copies:
        copy.wait()


def z_copy_to(zpart, zbuf, z_s, z_r, k, d, along):
    return remote(zpart.at[pl.ds(16 * k, 16)], zbuf.at[d - 1], z_s.at[k], z_r.at[d - 1], along(d))


def finish_call(s, wide):
    vm = pl.BlockSpec(memory_space=pltpu.VMEM)
    dma = pltpu.SemaphoreType.DMA
    return pl.pallas_call(
        finish_kernel,
        out_shape=(
            jax.ShapeDtypeStruct((8, 4, 96, 320), BF),
            jax.ShapeDtypeStruct((160, 360), BF),
        ),
        in_specs=[vm] * 2,
        out_specs=(vm, vm),
        scratch_shapes=[
            pltpu.VMEM((3, 96, 320), BF),
            pltpu.VMEM((96, 320), BF),
            pltpu.VMEM((15, 16, 320), BF),
            pltpu.VMEM((96, 320), BF),
            pltpu.VMEM((7, 160, 360), BF),
            dma((7,)),
            dma((7,)),
            dma((3,)),
            dma((3,)),
            dma((6,)),
            dma((15,)),
            dma((15,)),
            dma((6,)),
            dma((15,)),
            dma((15,)),
            dma((16,)),
            dma((16,)),
        ],
        compiler_params=pltpu.CompilerParams(
            collective_id=2, has_side_effects=True, vmem_limit_bytes=VMEM_BYTES
        ),
        name="finish_sums",
    )(s, wide)


def tap_columns(tangent):
    padded = jnp.pad(tangent, ((0, 0), (1, 1), (1, 1), (0, 0)))
    taps = []
    for a in range(3):
        for b in range(3):
            taps.append(padded[:, 2 - a : 16 - a, 2 - b : 16 - b, :])
    cols = jnp.concatenate(taps, axis=3)
    pieces = []
    blank = jnp.zeros((16, 360), BF)
    for u in range(8):
        h = (u + 1) % 8
        image, half = h // 2, h % 2
        rim = 6 if half == 1 else 7
        pieces.append(cols[image, 7 * half : 7 * half + 7].reshape(98, 360))
        pieces.append(cols[image, rim])
        pieces.append(blank)
    stacked = jnp.concatenate(pieces, axis=0).reshape(2, 4, 4, 32, 360)
    return stacked.transpose(1, 2, 0, 3, 4).reshape(4, 256, 360)


def local(
    narrow_input, narrow_output, narrow_mask, wide_cotangent, wide_mask, narrow_weight, wide_weight
):
    g, zh, y, x, c = place()
    j = 2 * x + c
    stacked = jnp.stack([narrow_output, narrow_mask.astype(BF), narrow_input])
    blk = jnp.pad(stacked, ((0, 0), (0, 15), (0, 0)))
    gath, halo, xall = gather_call(blk)

    tangent = wide_cotangent * wide_mask.astype(BF)
    tcol = tap_columns(tangent)
    wmat = wide_weight.transpose(0, 1, 3, 2).reshape(360, 1280)
    nb = reduce_call(tcol, wmat).reshape(2, 128, 640)

    odd = y % 2 == 1
    zero = jnp.zeros((), BF)
    above = jnp.where(odd, zero, halo[21:49])
    below = jnp.where(odd, halo[0:28], zero)
    mask = jnp.concatenate([above, gath[:, 1, :49].reshape(392, 320), below], axis=0)
    rows = gath[:, 2, :49].reshape(392, 320)
    inj = lax.dynamic_slice_in_dim(rows, 40 * j, 40, 1)
    s, ig = narrow_call(nb, mask, inj, narrow_weight.reshape(9, 320, 320))

    wide = lax.dot_general(
        xall.reshape(2, 1024, 640),
        tcol.reshape(1024, 360),
        (((1,), (0,)), ((), ())),
        preferred_element_type=F32,
    )
    wide = wide.reshape(8, 160, 360).astype(BF)
    ng, wg = finish_call(s.reshape(4, 96, 320), wide)
    narrow_gradient = (
        ng.reshape(8, 384, 320)[:, :360].reshape(8, 9, 40, 320).transpose(1, 0, 2, 3).reshape(3, 3, 320, 320)
    )
    wide_gradient = wg.T.reshape(3, 3, 40, 160).transpose(0, 1, 3, 2)
    return (narrow_gradient, wide_gradient, ig[:49])


def solution(mesh):
    placed = (
        P(("dp", "mp"), None),
        P(("dp", "mp"), None),
        P(("dp", "mp"), None),
        P("dp", None, None, "mp"),
        P("dp", None, None, "mp"),
        P(),
        P(None, None, None, "mp"),
    )
    return jax.shard_map(
        local,
        mesh=mesh,
        in_specs=placed,
        out_specs=(P(), P(None, None, "dp", "mp"), P(("dp", "mp"), None)),
        check_vma=False,
    )
```

time: 1580 us -> 228 us (0.14)
  the two profiles are of different devices: /device:TPU:6 before, /device:TPU:57 now
where the time goes in v1:
time: 228 us; the launch traced here: 227 us
  Pallas kernels  189 us (83%)
  local copies, waits for them, and re-layouts  29.6 us (13%)
  other arithmetic  4.56 us (2%)
  matrix products  3.3 us (1%)
    pallas_call x1, Pallas kernels, finish_call(): pl.pallas_call(finish_kernel, out_shape=(jax.ShapeDtypeStruct((8, 4, 96,...  79.9 us
    pallas_call x1, Pallas kernels, gather_call(): pl.pallas_call(gather_kernel, out_shape=(jax.ShapeDtypeStruct((8, 3, 64,...  55.6 us
    pallas_call x1, Pallas kernels, reduce_call(): pl.pallas_call(reduce_kernel, out_shape=jax.ShapeDtypeStruct((2, 4, 32, 6...  49.4 us
    unnamed x24, local copies, waits for them, and re-layouts  6.3 us
    concatenate x1, local copies, waits for them, and re-layouts, tap_columns(): cols = jnp.concatenate(taps, axis=3)  5.94 us

profile of v1, /device:TPU:57, one launch (start us, length us, event | category | flops | bytes accessed | tf_op | source)
XLA Modules:
  0.0 227.2 jit_solution(17872893151898086038)
XLA Ops:
  0.7 0.9 convert_bitcast_fusion
  1.6 0.8 fusion.4.blk
  2.4 1.1 convert_multiply_fusion
  3.6 0.5 pad_slice_fusion
  4.1 5.9 %concatenate.9 = bf16[4,14,14,360]{3,0,2,1:T(4,128)(2,1)S(1)} concatenate(bf16[4,14,14,40]{3,0,2,1:T(4,128)(2,1)S(1)} %get-tuple-element.42, bf16[4,14,14,40]{3,0,2,1:T(4,128)(2,1)S(1)} %get-tuple-element.36, bf16[4,14,14,40]{3,0,2,1:T(4,128)(2,1)S(1)} %get-tuple-element.37, bf16[4,14,14,40]{3,0,2,1:T(4,128)(2,1)S(1)} %get-tuple-element.38, bf16[4,14,14,40]{3,0,2,1:T(4,128)(2,1)S(1)} %bitcast.65, ...), dimensions={3} | concatenate | bytes 1128960 | tf_op jit(solution)/shard_map/concatenate | solution.py:592
  10.0 0.1 fusion.6
  10.2 3.2 %slice_reduce_fusion = (bf16[7,14,360]{2,1,0:T(8,128)(2,1)S(1)}, bf16[7,14,360]{2,1,0:T(8,128)(2,1)S(1)}, bf16[7,14,360]{2,1,0:T(8,128)(2,1)S(1)}, bf16[7,14,360...) fusion(bf16[4,14,14,360]{3,0,2,1:T(4,128)(2,1)S(1)} %concatenate.9), kind=kLoop, calls=%fused_computation.7 | loop fusion | bytes 1128960 | tf_op jit(solution)/shard_map/slice | solution.py:599
  13.4 0.0 copy-start.4
  13.7 1.5 concatenate.10
  15.2 0.0 copy-start.5
  15.2 0.0 copy-start.6
  15.2 0.1 copy.26
  15.3 0.0 copy-done.4
  15.4 49.4 %reduce_back.1 = bf16[2,4,32,640]{3,2,1,0:T(8,128)(2,1)S(1)} custom-call(bf16[4,256,360]{2,1,0:T(8,128)(2,1)S(1)} %bitcast.51, bf16[360,1280]{1,0:T(8,128)(2,1)S(1)} %bitcast.57), custom_call_target="tpu_custom_call" | custom-call | tf_op jit(solution)/shard_map/reduce_back/pallas_call | solution.py:316
  64.7 0.0 copy-start.1
  64.8 0.7 copy-done.1
  65.5 0.0 copy-done.5
  65.5 0.0 copy-done.6
  65.5 55.6 %gather_rows.1 = (bf16[8,3,64,320]{3,2,1,0:T(8,128)(2,1)S(1)}, bf16[64,320]{1,0:T(8,128)(2,1)S(1)}, bf16[2,4,4,2,32,640]{5,4,3,2,1,0:T(8,128)(2,1)S(1)}) custom-call(bf16[3,64,320]{2,1,0:T(8,128)(2,1)S(1)} %fusion.4.blk, bf16[4,128,512]{2,1,0:T(8,128)(2,1)S(1)} %copy-done.6, bf16[2,320,640]{2,1,0:T(8,128)(2,1)S(1)} %copy-done.5), custom_call_target="tpu_custom_call" | custom-call | tf_op jit(solution)/shard_map/gather_rows/pallas_call | solution.py:195
  121.0 0.6 slice_select_fusion.1
  121.7 0.9 fusion.5
  122.6 1.8 reshape_squeeze.39
  124.4 1.0 constant_dynamic-slice_fusion.inj
  125.4 1.8 reshape_squeeze.38
  127.3 1.1 pad_maximum_fusion.mask
  128.3 0.0 copy-start
  128.4 1.6 copy-done
  130.0 0.0 copy-start.2
  130.0 1.0 copy-done.2
  131.0 0.0 copy-start.3
  131.0 1.2 copy-done.3
  132.2 0.0 copy-start.7
  132.2 1.0 copy-done.7
  133.2 3.8 %narrow_local.1 = (bf16[384,320]{1,0:T(8,128)(2,1)S(1)}, bf16[64,320]{1,0:T(8,128)(2,1)S(1)}) custom-call(bf16[2,128,640]{2,1,0:T(8,128)(2,1)S(1)} %bitcast.56, bf16[448,320]{1,0:T(8,128)(2,1)S(1)} %pad_maximum_fusion.mask, bf16[392,40]{1,0:T(8,128)(2,1)S(1)} %constant_dynamic-slice_fusion.inj, bf16[9,320,320]{2,1,0:T(8,128)(2,1)S(1)} %bitcast.54, ...), custom_call_target="tpu_custom_call" | custom-call | tf_op jit(solution)/shard_map/narrow_local/pallas_call | solution.py:386
  137.0 0.0 copy-start.8
  137.0 0.7 copy-done.8
  137.7 0.6 slice.120
  138.4 2.8 %copy.27 = bf16[2,640,1024]{2,1,0:T(8,128)(2,1)} copy(bf16[2,640,1024]{1,2,0:T(8,128)(2,1)S(1)} %bitcast.53) | data formatting | bytes 5242880 | tf_op jit(solution)/shard_map/dot_general | solution.py:629
  141.1 0.0 copy-start.9
  141.1 3.3 %convolution_convert_fusion.wide = bf16[8,160,360]{2,1,0:T(8,128)(2,1)S(1)} fusion(bf16[8,160,1024]{2,1,0:T(8,128)(2,1)} %bitcast.62, bf16[1024,360,1]{1,0,2:T(8,128)(2,1)S(1)} %bitcast.52), kind=kOutput, calls=%fused_computation | convolution fusion | flops 944179200 | bytes 4280320 | tf_op jit(solution)/shard_map/dot_general | solution.py:629
  144.5 0.0 copy-done.9
  144.5 79.9 %finish_sums.1 = (bf16[8,4,96,320]{3,2,1,0:T(8,128)(2,1)S(1)}, bf16[160,360]{1,0:T(8,128)(2,1)S(1)}) custom-call(bf16[4,96,320]{2,1,0:T(8,128)(2,1)S(1)} %bitcast.58, bf16[8,160,360]{2,1,0:T(8,128)(2,1)S(1)} %convolution_convert_fusion.wide), custom_call_target="tpu_custom_call" | custom-call | tf_op jit(solution)/shard_map/finish_sums/pallas_call | solution.py:552
  224.4 0.2 slice.137
  224.7 1.7 copy.30
  226.3 0.8 copy.31
  (13 shorter events, 0.4 us)
Async XLA Ops:
  13.4 2.0 copy-start.4
  15.2 50.3 %copy-start.5 = (bf16[2,320,640]{2,1,0:T(8,128)(2,1)S(1)}, bf16[2,320,640]{2,1,0:T(8,128)(2,1)}, u32[]{:S(2)}) copy-start(bf16[2,320,640]{2,1,0:T(8,128)(2,1)} %constant.75.clone.put) | copy-start | bytes 2457604
  15.2 50.3 %copy-start.6 = (bf16[4,128,512]{2,1,0:T(8,128)(2,1)S(1)}, bf16[4,128,512]{2,1,0:T(8,128)(2,1)}, u32[]{:S(2)}) copy-start(bf16[4,128,512]{2,1,0:T(8,128)(2,1)} %constant.74.clone.perm) | copy-start | bytes 1572868
  64.7 0.7 copy-start.1
  128.3 1.6 copy-start
  130.0 1.0 copy-start.2
  131.0 1.2 copy-start.3
  132.2 1.0 copy-start.7
  137.0 0.7 copy-start.8
  141.1 3.3 %copy-start.9 = (bf16[384,320]{1,0:T(8,128)(2,1)S(1)}, bf16[384,320]{1,0:T(8,128)(2,1)}, u32[]{:S(2)}) copy-start(bf16[384,320]{1,0:T(8,128)(2,1)} %copy-done.8) | copy-start | bytes 737284
